TPU v7x, 512 devices: a whole 4x8x8 slice. The times are simulated.
512 devices in a mesh: list: 16 (over z, core), sub: 8 (over y), slab: 4 (over x).
Axes of the slice: x: 4, y: 8, z: 8, core: 2. Of those that a mesh axis runs over, the one named last changes fastest.
Arguments:
- vectors: float32 [1024, 65536], P(None, ('list', 'sub', 'slab')), may hold values from -10 to 10
- centroids: bfloat16 [1024, 262144], P('sub', ('list', 'slab')), may hold values from -3 to 3
- codebook: float32 [32, 256, 32], P('sub'), may hold values from -10 to 10
- list_ids: int32 [65536], P(('list', 'sub', 'slab')), may hold values from 0 to 262143, as said below
Outputs:
- fresh_codebook: float32 [32, 256, 32], P('sub')
Inputs may be any that keep to these rules, and one draw needn't show every extreme that they name: `list_ids`: among the columns of one device, at most 4 name lists of one owner (list id // 4096); in every draw one owner receives exactly 4 from every device.
All inputs are finite; a program needn't handle non-finite values.
Results may differ from a plain program's by a relative error of at most 0.0003.
Values sent between devices are 32-bit elements; how exact they have to be, the bound alone decides.
A program may use at most 64 MiB of HBM per device.

v0:
```python
import math
import jax
import jax.numpy as jnp
from jax import lax
from jax.sharding import PartitionSpec as P

SOFTMAX_HEAT = 8.0
PRIOR_MASS = 1.0


def owner_rank(owner_of, owners):
    row_count = owner_of.shape[0]
    matches = (owner_of[:, None] == jnp.arange(owners)[None, :]).astype(jnp.float32)
    block = math.gcd(row_count, 128)
    blocks = matches.reshape(row_count // block, block, owners)
    strict_lower = (jnp.arange(block)[:, None] > jnp.arange(block)[None, :]).astype(jnp.float32)
    inside = jnp.einsum("ij,bjo->bio", strict_lower, blocks)
    totals = jnp.sum(blocks, axis=1)
    before = jnp.cumsum(totals, axis=0) - totals
    ranking = (inside + before[:, None, :]).reshape(row_count, owners)
    return jnp.sum(ranking * matches, axis=1).astype(jnp.int32)


def soft_sums(residual, weight, codebook):
    groups, num_codes, width = codebook.shape
    total_columns = residual.shape[1]
    block = math.gcd(total_columns, 1024)
    codeword_norm = jnp.sum(codebook * codebook, axis=-1)

    def block_step(loop_index, running):
        counts, weighted = running
        offset = (loop_index * block).astype(jnp.int32)
        column_piece = lax.dynamic_slice_in_dim(residual, offset, block, 1).reshape(
            groups, width, block
        )
        present = lax.dynamic_slice_in_dim(weight, offset, block, 0)
        inner_products = jnp.einsum(
            "skd,sdn->skn", codebook, column_piece, precision=lax.Precision.HIGHEST
        )
        assignment_scores = (2.0 * inner_products - codeword_norm[:, :, None]) / SOFTMAX_HEAT
        assignment_scores = assignment_scores - jnp.max(assignment_scores, axis=1, keepdims=True)
        exponent = jnp.exp(assignment_scores)
        assign = exponent / jnp.sum(exponent, axis=1, keepdims=True) * present[None, None, :]
        counts = counts + jnp.sum(assign, axis=2)
        weighted = weighted + jnp.einsum(
            "skn,sdn->skd", assign, column_piece, precision=lax.Precision.HIGHEST
        )
        return (counts, weighted)

    start_state = (
        jnp.zeros((groups, num_codes), jnp.float32),
        jnp.zeros((groups, num_codes, width), jnp.float32),
    )
    return lax.fori_loop(0, total_columns // block, block_step, start_state)


def refresh(counts, weighted, previous):
    return (weighted + PRIOR_MASS * previous) / (counts[:, :, None] + PRIOR_MASS)


def per_device(vectors, centroids, codebook, list_ids):
    list_count = lax.axis_size("list")
    slab_count = lax.axis_size("slab")
    sub_count = lax.axis_size("sub")
    owners = list_count * slab_count
    lists_here = centroids.shape[1]
    row_count = vectors.shape[1]
    capacity = 2 * row_count // owners
    owner_of = list_ids // lists_here
    within = (list_ids % lists_here).astype(jnp.float32)
    slot = owner_of * capacity + owner_rank(owner_of, owners)
    packed = jnp.zeros((vectors.shape[0], owners * capacity), jnp.float32).at[:, slot].set(vectors)
    labels = jnp.full((owners * capacity,), -1.0, jnp.float32).at[slot].set(within)
    labels = jnp.broadcast_to(labels[None, :], (sub_count, owners * capacity))
    arrived, arrived_labels = (
        lax.all_to_all(packed, ("list", "slab"), split_axis=1, concat_axis=1, tiled=True),
        lax.all_to_all(labels, ("list", "slab"), split_axis=1, concat_axis=1, tiled=True),
    )
    columns, column_labels = (
        lax.all_to_all(arrived, "sub", split_axis=0, concat_axis=1, tiled=True),
        lax.all_to_all(arrived_labels, "sub", split_axis=0, concat_axis=1, tiled=True),
    )
    final_labels = column_labels[0]
    present = final_labels >= 0.0
    weight = present.astype(jnp.float32)
    list_index = jnp.where(present, final_labels, 0.0).astype(jnp.int32)
    nearest = jnp.take(centroids, list_index, axis=1).astype(jnp.float32)
    residual = (columns - nearest) * weight[None, :]
    counts, weighted = soft_sums(residual, weight, codebook)
    counts, weighted = lax.psum((counts, weighted), ("list", "slab"))
    return refresh(counts, weighted, codebook)


def solution(mesh):
    return jax.shard_map(
        per_device,
        mesh=mesh,
        in_specs=(
            P(None, ("list", "sub", "slab")),
            P("sub", ("list", "slab")),
            P("sub", None, None),
            P(("list", "sub", "slab")),
        ),
        out_specs=P("sub", None, None),
        check_vma=False,
    )
```

profile of v0, /device:TPU:1, one launch (start us, length us, event | category | flops | bytes accessed | tf_op | source)
XLA Modules:
  0.0 453.4 jit_solution(12421118974912579844)
XLA Ops:
  7.5 1.0 scatter_custom_fusion.1
  9.4 14.8 %all-to-all-start.2 = ((f32[8,64,4]{0,2,1:T(4,128)}), f32[8,64,4]{0,2,1:T(4,128)S(1)}, u32[]{:S(2)}, u32[]{:S(2)}) async-start(f32[8,64,4]{0,2,1:T(4,128)} %broadcast_in_dim.61), calls=%async_computation.2 | async-start | bytes 262144 | tf_op jit(solution)/shard_map/all_to_all | solution.py:77
  24.2 1.2 copy.24
  25.5 1.3 scatter_custom_fusion
  26.8 1.3 all_to_all.34
  28.1 6.1 %all-to-all-done.2 = f32[8,64,4]{0,2,1:T(4,128)S(1)} async-done(((f32[8,64,4]{0,2,1:T(4,128)}), f32[8,64,4]{0,2,1:T(4,128)S(1)}, u32[]{:S(2)}, u32[]{:S(2)}) %all-to-all-start.2) | async-done | bytes 8224 | tf_op jit(solution)/shard_map/all_to_all | solution.py:77
  34.2 6.0 %all-to-all-start = ((f32[1024,64,4]{0,2,1:T(4,128)}), f32[1024,64,4]{0,2,1:T(4,128)S(1)}, u32[]{:S(2)}, u32[]{:S(2)}) async-start(f32[1024,64,4]{0,2,1:T(4,128)} %all_to_all.34), calls=%async_computation | async-start | bytes 2097152 | tf_op jit(solution)/shard_map/all_to_all | solution.py:76
  40.8 27.1 %all-to-all-done = f32[1024,64,4]{0,2,1:T(4,128)S(1)} async-done(((f32[1024,64,4]{0,2,1:T(4,128)}), f32[1024,64,4]{0,2,1:T(4,128)S(1)}, u32[]{:S(2)}, u32[]{:S(2)}) %all-to-all-start) | async-done | bytes 1048608 | tf_op jit(solution)/shard_map/all_to_all | solution.py:76
  68.0 6.8 %all-to-all-start.3 = ((f32[8,1,256]{2,1,0:T(1,128)}), f32[8,1,256]{2,1,0:T(1,128)S(1)}, u32[]{:S(2)}, u32[]{:S(2)}) async-start(f32[8,1,256]{2,1,0:T(1,128)} %copy.26), calls=%async_computation.3 | async-start | bytes 16384 | tf_op jit(solution)/shard_map/all_to_all | solution.py:81
  75.2 1.2 copy.25
  76.4 5.0 %all-to-all-done.3 = f32[8,1,256]{2,1,0:T(1,128)S(1)} async-done(((f32[8,1,256]{2,1,0:T(1,128)}), f32[8,1,256]{2,1,0:T(1,128)S(1)}, u32[]{:S(2)}, u32[]{:S(2)}) %all-to-all-start.3) | async-done | bytes 8224 | tf_op jit(solution)/shard_map/all_to_all | solution.py:81
  81.4 3.6 all-to-all-start.1
  85.9 6.2 %gather_fusion = bf16[2048,128]{1,0:T(8,128)(2,1)S(1)} fusion(bf16[128,4096]{0,1:T(8,128)(2,1)S(1)} %copy.27, s32[2048]{0:T(1024)S(1)} %broadcast_clamp_fusion), kind=kCustom, calls=%fused_computation | custom fusion | bytes 1056768 | tf_op jit(solution)/shard_map/jit(_take)/gather | solution.py:87
  92.1 19.6 %all-to-all-done.1 = f32[8,128,256]{1,2,0:T(8,128)S(1)} async-done(((f32[8,128,256]{1,2,0:T(8,128)}), f32[8,128,256]{1,2,0:T(8,128)S(1)}, u32[]{:S(2)}, u32[]{:S(2)}) %all-to-all-start.1) | async-done | bytes 1048608 | tf_op jit(solution)/shard_map/all_to_all | solution.py:80
  112.5 27.6 %while.16 = (s32[]{:T(128)}, f32[4,256]{1,0:T(4,128)S(1)}, f32[4,256,32]{1,2,0:T(8,128)S(1)}, f32[128,2048]{0,1:T(8,128)S(1)}, f32[4,256,32]{1,2,0:T(8,128)S(1)}...) while((s32[]{:T(128)}, f32[4,256]{1,0:T(4,128)S(1)}, ...), condition=%wide.region_9.10_spmd.clone, body=%wide.region_5.9_spmd.clone.sunk | while | flops 819004672 | bytes 41373896 | solution.py:54
  112.8 3.5 fusion.41
  116.2 3.0 fusion.42
  119.2 6.5 %fusion.44 = f32[4,256,32]{1,2,0:T(8,128)S(1)} fusion(f32[4,32,1024]{2,1,0:T(8,128)S(1)} %bitcast.61, f32[4,256,1024]{2,1,0:T(8,128)} %get-tuple-element.256, f32[1024]{0:T(1024)S(1)} %dynamic_slice.20, f32[4,1024]{1,0:T(4,128)S(1)} %get-tuple-element.257, f32[4,256,32]{1,2,0:T(8,128)S(1)} %get-tuple-element.271, pred[]{:T(512)S(6)} %compare.6), kind=kOutput, calls=%fused_computation.15.clone.1 | convolution fusion | flops 404815872 | bytes 5001217 | tf_op jit(solution)/shard_map/while/body/eval_jaxpr/skn,sdn->skd/dot_general | solution.py:45
  126.6 3.5 fusion.41
  130.0 3.0 fusion.42
  133.0 6.5 %fusion.44 = f32[4,256,32]{1,2,0:T(8,128)S(1)} fusion(f32[4,32,1024]{2,1,0:T(8,128)S(1)} %bitcast.61, f32[4,256,1024]{2,1,0:T(8,128)} %get-tuple-element.256, f32[1024]{0:T(1024)S(1)} %dynamic_slice.20, f32[4,1024]{1,0:T(4,128)S(1)} %get-tuple-element.257, f32[4,256,32]{1,2,0:T(8,128)S(1)} %get-tuple-element.271, pred[]{:T(512)S(6)} %compare.6), kind=kOutput, calls=%fused_computation.15.clone.1 | convolution fusion | flops 404815872 | bytes 5001217 | tf_op jit(solution)/shard_map/while/body/eval_jaxpr/skn,sdn->skd/dot_general | solution.py:45
  140.1 123.2 %psum.15 = f32[4,256]{1,0:T(4,128)S(1)} all-reduce(f32[4,256]{1,0:T(4,128)S(1)} %get-tuple-element.131), channel_id=1, replica_groups=mesh['list'=16,'sub'=8,'slab'=4] {'list','slab'}, use_global_device_ids=true, to_apply=%region_11.12 | all-reduce | flops 1024 | bytes 8192 | tf_op jit(solution)/shard_map/psum | solution.py:90
  263.4 181.7 %all-reduce.2.cloned.1.call-done = f32[4,256,32]{1,2,0:T(8,128)} async-done(((f32[4,256,32]{1,2,0:T(8,128)}), f32[4,256,32]{1,2,0:T(8,128)}) %all-reduce.2.cloned.1.call-update) | async-done | bytes 131088 | tf_op jit(solution)/shard_map/psum | solution.py:90
  445.0 1.6 add_divide_fusion
  (40 shorter events, 6.2 us)
Async XLA Ops:
  9.4 24.8 %all-to-all-start.2 = ((f32[8,64,4]{0,2,1:T(4,128)}), f32[8,64,4]{0,2,1:T(4,128)S(1)}, u32[]{:S(2)}, u32[]{:S(2)}) async-start(f32[8,64,4]{0,2,1:T(4,128)} %broadcast_in_dim.61), calls=%async_computation.2 | async-start | bytes 262144 | tf_op jit(solution)/shard_map/all_to_all | solution.py:77
  28.1 57.1 %copy-start.2 = (bf16[128,4096]{1,0:T(8,128)(2,1)S(1)}, bf16[128,4096]{1,0:T(8,128)(2,1)}, u32[]{:S(2)}) copy-start(bf16[128,4096]{1,0:T(8,128)(2,1)} %param.7) | copy-start | bytes 3145732
  34.2 33.8 %all-to-all-start = ((f32[1024,64,4]{0,2,1:T(4,128)}), f32[1024,64,4]{0,2,1:T(4,128)S(1)}, u32[]{:S(2)}, u32[]{:S(2)}) async-start(f32[1024,64,4]{0,2,1:T(4,128)} %all_to_all.34), calls=%async_computation | async-start | bytes 2097152 | tf_op jit(solution)/shard_map/all_to_all | solution.py:76
  68.0 13.4 %all-to-all-start.3 = ((f32[8,1,256]{2,1,0:T(1,128)}), f32[8,1,256]{2,1,0:T(1,128)S(1)}, u32[]{:S(2)}, u32[]{:S(2)}) async-start(f32[8,1,256]{2,1,0:T(1,128)} %copy.26), calls=%async_computation.3 | async-start | bytes 16384 | tf_op jit(solution)/shard_map/all_to_all | solution.py:81
  74.8 11.1 %copy-start.1 = (f32[4,256,32]{1,2,0:T(8,128)S(1)}, f32[4,256,32]{1,2,0:T(8,128)}, u32[]{:S(2)}) copy-start(f32[4,256,32]{1,2,0:T(8,128)} %param.8) | copy-start | bytes 393220
  81.4 30.4 %all-to-all-start.1 = ((f32[8,128,256]{1,2,0:T(8,128)}), f32[8,128,256]{1,2,0:T(8,128)S(1)}, u32[]{:S(2)}, u32[]{:S(2)}) async-start(f32[8,128,256]{1,2,0:T(8,128)} %copy.25), calls=%async_computation.1 | async-start | bytes 2097152 | tf_op jit(solution)/shard_map/all_to_all | solution.py:80
  84.9 360.1 %all-reduce.2.cloned.1.call-start = ((), (), s32[]{:S(2)}) async-start(), calls=%async_computation.4 | async-start | bytes 262144 | tf_op jit(solution)/shard_map/psum | solution.py:90
  119.2 6.5 %copy-start = (f32[4,256,1024]{2,1,0:T(8,128)S(1)}, f32[4,256,1024]{2,1,0:T(8,128)}, u32[]{:S(2)}) copy-start(f32[4,256,1024]{2,1,0:T(8,128)} %get-tuple-element.256) | copy-start | bytes 12582916 | tf_op jit(solution)/shard_map/while
  133.0 6.5 %copy-start = (f32[4,256,1024]{2,1,0:T(8,128)S(1)}, f32[4,256,1024]{2,1,0:T(8,128)}, u32[]{:S(2)}) copy-start(f32[4,256,1024]{2,1,0:T(8,128)} %get-tuple-element.256) | copy-start | bytes 12582916 | tf_op jit(solution)/shard_map/while
  140.1 123.2 %copy-start.3 = (f32[4,256,32]{1,2,0:T(8,128)}, f32[4,256,32]{1,2,0:T(8,128)S(1)}, u32[]{:S(2)}) copy-start(f32[4,256,32]{1,2,0:T(8,128)S(1)} %get-tuple-element.130) | copy-start | bytes 393220
Sparse Core Ops, SparseCore 0:
  263.5 181.4 all-reduce.1
where the time goes:
time: 454 us; the launch traced here: 453 us
  waiting for transfers between devices  239 us (53%)
  blocking collectives  123 us (27%)
  starting transfers between devices  31.4 us (7%)
  matrix products  20.1 us (4%)
  local copies, waits for them, and re-layouts  15.3 us (3%)
  between operations  13.6 us (3%)
  other arithmetic  10.2 us (2%)
    psum x1, waiting for transfers between devices, per_device(): counts, weighted = lax.psum((counts, weighted), ('list', 'slab'))  182 us
    psum x1, blocking collectives, per_device(): counts, weighted = lax.psum((counts, weighted), ('list', 'slab'))  123 us
    all_to_all x1, waiting for transfers between devices, per_device(): lax.all_to_all(packed, ('list', 'slab'), split_axis=1, concat_axis=1, til...  27.1 us
    all_to_all x1, waiting for transfers between devices, per_device(): lax.all_to_all(arrived, 'sub', split_axis=0, concat_axis=1, tiled=True)  19.6 us
    all_to_all x1, starting transfers between devices, per_device(): lax.all_to_all(labels, ('list', 'slab'), split_axis=1, concat_axis=1, til...  14.8 us
    dot_general x2, matrix products, block_step(): jnp.einsum('skn,sdn->skd', assign, column_piece, precision=lax.Precision....  13 us
  transfers between devices with their start and end apart: 5, of which 5 were waited for; matrix products, arithmetic and copies ran while one was open for 2% of the time, Pallas kernels for 0%

commit v1 on v0

--- a/solution.py
+++ b/solution.py
@@ -87,7 +87,7 @@
     nearest = jnp.take(centroids, list_index, axis=1).astype(jnp.float32)
     residual = (columns - nearest) * weight[None, :]
     counts, weighted = soft_sums(residual, weight, codebook)
-    counts, weighted = lax.psum((counts, weighted), ("list", "slab"))
+    counts, weighted = lax.psum(lax.psum((counts, weighted), "list"), "slab")
     return refresh(counts, weighted, codebook)
 
 

time: 454 us -> 311 us (0.69)
  blocking collectives: 123 us -> 34 us
  waiting for transfers between devices: 239 us -> 184 us
    psum x1 -> x2, blocking collectives: 123 us -> 34 us  [per_device(): counts, weighted = lax.psum(lax.psum((counts, weighted), 'list'), 'slab')]
    psum x1 -> x2, waiting for transfers between devices: 182 us -> 126 us  [per_device(): counts, weighted = lax.psum(lax.psum((counts, weighted), 'list'), 'slab')]
  transfers between devices with their start and end apart: 5 -> 6, of which waited for: 5 -> 6; matrix products, arithmetic and copies ran while one was open for 2% -> 4% of each run, Pallas kernels for 0% -> 0%
where the time goes in v1:
time: 311 us; the launch traced here: 310 us
  waiting for transfers between devices  184 us (59%)
  blocking collectives  34 us (11%)
  starting transfers between devices  31.5 us (10%)
  matrix products  20.1 us (6%)
  local copies, waits for them, and re-layouts  15.9 us (5%)
  between operations  13.6 us (4%)
  other arithmetic  10.2 us (3%)
    psum x2, waiting for transfers between devices, per_device(): counts, weighted = lax.psum(lax.psum((counts, weighted), 'list'), 'slab')  126 us
    psum x2, blocking collectives, per_device(): counts, weighted = lax.psum(lax.psum((counts, weighted), 'list'), 'slab')  34 us
    all_to_all x1, waiting for transfers between devices, per_device(): lax.all_to_all(packed, ('list', 'slab'), split_axis=1, concat_axis=1, til...  27.1 us
    all_to_all x1, waiting for transfers between devices, per_device(): lax.all_to_all(arrived, 'sub', split_axis=0, concat_axis=1, tiled=True)  19.6 us
    all_to_all x1, starting transfers between devices, per_device(): lax.all_to_all(labels, ('list', 'slab'), split_axis=1, concat_axis=1, til...  14.8 us
    dot_general x2, matrix products, block_step(): jnp.einsum('skn,sdn->skd', assign, column_piece, precision=lax.Precision....  13 us
    dot_general x2, matrix products, block_step(): jnp.einsum('skd,sdn->skn', codebook, column_piece, precision=lax.Precisio...  6.92 us
    all_to_all x1, starting transfers between devices, per_device(): lax.all_to_all(arrived_labels, 'sub', split_axis=0, concat_axis=1, tiled=...  6.82 us
  transfers between devices with their start and end apart: 6, of which 6 were waited for; matrix products, arithmetic and copies ran while one was open for 4% of the time, Pallas kernels for 0%

profile of v1, /device:TPU:1, one launch (start us, length us, event | category | flops | bytes accessed | tf_op | source)
XLA Modules:
  0.0 309.6 jit_solution(15459681026933057030)
XLA Ops:
  9.4 14.8 %all-to-all-start.2 = ((f32[8,64,4]{0,2,1:T(4,128)}), f32[8,64,4]{0,2,1:T(4,128)S(1)}, u32[]{:S(2)}, u32[]{:S(2)}) async-start(f32[8,64,4]{0,2,1:T(4,128)} %broadcast_in_dim.61), calls=%async_computation.2 | async-start | bytes 262144 | tf_op jit(solution)/shard_map/all_to_all | solution.py:77
  24.2 1.2 copy.24
  25.5 1.3 scatter_custom_fusion
  26.8 1.3 all_to_all.34
  28.1 6.1 %all-to-all-done.2 = f32[8,64,4]{0,2,1:T(4,128)S(1)} async-done(((f32[8,64,4]{0,2,1:T(4,128)}), f32[8,64,4]{0,2,1:T(4,128)S(1)}, u32[]{:S(2)}, u32[]{:S(2)}) %all-to-all-start.2) | async-done | bytes 8224 | tf_op jit(solution)/shard_map/all_to_all | solution.py:77
  34.2 6.0 %all-to-all-start = ((f32[1024,64,4]{0,2,1:T(4,128)}), f32[1024,64,4]{0,2,1:T(4,128)S(1)}, u32[]{:S(2)}, u32[]{:S(2)}) async-start(f32[1024,64,4]{0,2,1:T(4,128)} %all_to_all.34), calls=%async_computation | async-start | bytes 2097152 | tf_op jit(solution)/shard_map/all_to_all | solution.py:76
  40.8 27.1 %all-to-all-done = f32[1024,64,4]{0,2,1:T(4,128)S(1)} async-done(((f32[1024,64,4]{0,2,1:T(4,128)}), f32[1024,64,4]{0,2,1:T(4,128)S(1)}, u32[]{:S(2)}, u32[]{:S(2)}) %all-to-all-start) | async-done | bytes 1048608 | tf_op jit(solution)/shard_map/all_to_all | solution.py:76
  68.0 6.8 %all-to-all-start.3 = ((f32[8,1,256]{2,1,0:T(1,128)}), f32[8,1,256]{2,1,0:T(1,128)S(1)}, u32[]{:S(2)}, u32[]{:S(2)}) async-start(f32[8,1,256]{2,1,0:T(1,128)} %copy.26), calls=%async_computation.3 | async-start | bytes 16384 | tf_op jit(solution)/shard_map/all_to_all | solution.py:81
  76.4 5.0 %all-to-all-done.3 = f32[8,1,256]{2,1,0:T(1,128)S(1)} async-done(((f32[8,1,256]{2,1,0:T(1,128)}), f32[8,1,256]{2,1,0:T(1,128)S(1)}, u32[]{:S(2)}, u32[]{:S(2)}) %all-to-all-start.3) | async-done | bytes 8224 | tf_op jit(solution)/shard_map/all_to_all | solution.py:81
  81.4 3.6 %all-to-all-start.1 = ((f32[8,128,256]{1,2,0:T(8,128)}), f32[8,128,256]{1,2,0:T(8,128)S(1)}, u32[]{:S(2)}, u32[]{:S(2)}) async-start(f32[8,128,256]{1,2,0:T(8,128)} %copy.25), calls=%async_computation.1 | async-start | bytes 2097152 | tf_op jit(solution)/shard_map/all_to_all | solution.py:80
  85.9 6.2 %gather_fusion = bf16[2048,128]{1,0:T(8,128)(2,1)S(1)} fusion(bf16[128,4096]{0,1:T(8,128)(2,1)S(1)} %copy.27, s32[2048]{0:T(1024)S(1)} %broadcast_clamp_fusion), kind=kCustom, calls=%fused_computation | custom fusion | bytes 1056768 | tf_op jit(solution)/shard_map/jit(_take)/gather | solution.py:87
  92.1 19.6 %all-to-all-done.1 = f32[8,128,256]{1,2,0:T(8,128)S(1)} async-done(((f32[8,128,256]{1,2,0:T(8,128)}), f32[8,128,256]{1,2,0:T(8,128)S(1)}, u32[]{:S(2)}, u32[]{:S(2)}) %all-to-all-start.1) | async-done | bytes 1048608 | tf_op jit(solution)/shard_map/all_to_all | solution.py:80
  112.5 27.6 %while.16 = (s32[]{:T(128)}, f32[4,256]{1,0:T(4,128)S(1)}, f32[4,256,32]{1,2,0:T(8,128)S(1)}, f32[128,2048]{0,1:T(8,128)S(1)}, f32[4,256,32]{1,2,0:T(8,128)S(1)}...) while((s32[]{:T(128)}, f32[4,256]{1,0:T(4,128)S(1)}, ...), condition=%wide.region_9.10_spmd.clone, body=%wide.region_5.9_spmd.clone.sunk | while | flops 819004672 | bytes 41373896 | solution.py:54
  112.8 3.5 %fusion.41 = f32[4,1024,256]{1,2,0:T(8,128)S(1)} fusion(f32[4,32,1024]{2,1,0:T(8,128)S(1)} %bitcast.60, f32[4,256,32]{1,2,0:T(8,128)S(1)} %get-tuple-element.284), kind=kOutput, calls=%fused_computation.56.clone.1 | convolution fusion | flops 402653184 | bytes 4849664 | tf_op jit(solution)/shard_map/while/body/eval_jaxpr/skd,sdn->skn/dot_general | solution.py:37
  116.2 3.0 fusion.42
  119.2 6.5 %fusion.44 = f32[4,256,32]{1,2,0:T(8,128)S(1)} fusion(f32[4,32,1024]{2,1,0:T(8,128)S(1)} %bitcast.61, f32[4,256,1024]{2,1,0:T(8,128)} %get-tuple-element.256, f32[1024]{0:T(1024)S(1)} %dynamic_slice.20, f32[4,1024]{1,0:T(4,128)S(1)} %get-tuple-element.257, f32[4,256,32]{1,2,0:T(8,128)S(1)} %get-tuple-element.271, pred[]{:T(512)S(6)} %compare.6), kind=kOutput, calls=%fused_computation.15.clone.1 | convolution fusion | flops 404815872 | bytes 5001217 | tf_op jit(solution)/shard_map/while/body/eval_jaxpr/skn,sdn->skd/dot_general | solution.py:45
  126.6 3.5 %fusion.41 = f32[4,1024,256]{1,2,0:T(8,128)S(1)} fusion(f32[4,32,1024]{2,1,0:T(8,128)S(1)} %bitcast.60, f32[4,256,32]{1,2,0:T(8,128)S(1)} %get-tuple-element.284), kind=kOutput, calls=%fused_computation.56.clone.1 | convolution fusion | flops 402653184 | bytes 4849664 | tf_op jit(solution)/shard_map/while/body/eval_jaxpr/skd,sdn->skn/dot_general | solution.py:37
  130.0 3.0 fusion.42
  133.0 6.5 %fusion.44 = f32[4,256,32]{1,2,0:T(8,128)S(1)} fusion(f32[4,32,1024]{2,1,0:T(8,128)S(1)} %bitcast.61, f32[4,256,1024]{2,1,0:T(8,128)} %get-tuple-element.256, f32[1024]{0:T(1024)S(1)} %dynamic_slice.20, f32[4,1024]{1,0:T(4,128)S(1)} %get-tuple-element.257, f32[4,256,32]{1,2,0:T(8,128)S(1)} %get-tuple-element.271, pred[]{:T(512)S(6)} %compare.6), kind=kOutput, calls=%fused_computation.15.clone.1 | convolution fusion | flops 404815872 | bytes 5001217 | tf_op jit(solution)/shard_map/while/body/eval_jaxpr/skn,sdn->skd/dot_general | solution.py:45
  140.8 25.8 %psum.30 = f32[4,256]{1,0:T(4,128)S(1)} all-reduce(f32[4,256]{1,0:T(4,128)S(1)} %get-tuple-element.131), channel_id=1, replica_groups=mesh['list'=16,'sub'=8,'slab'=4] {'list'}, use_global_device_ids=true, to_apply=%region_12.13 | all-reduce | flops 1024 | bytes 8192 | tf_op jit(solution)/shard_map/psum | solution.py:90
  166.6 8.3 %psum.31 = f32[4,256]{1,0:T(4,128)S(1)} all-reduce(f32[4,256]{1,0:T(4,128)S(1)} %psum.30), channel_id=1, replica_groups=mesh['list'=16,'sub'=8,'slab'=4] {'slab'}, use_global_device_ids=true, to_apply=%region_13.14 | all-reduce | flops 1024 | bytes 8192 | tf_op jit(solution)/shard_map/psum | solution.py:90
  174.9 74.4 %all-reduce.3.cloned.1.call-done = f32[4,256,32]{1,2,0:T(8,128)} async-done(((f32[4,256,32]{1,2,0:T(8,128)}), f32[4,256,32]{1,2,0:T(8,128)}) %all-reduce.3.cloned.1.call-update) | async-done | bytes 131088 | tf_op jit(solution)/shard_map/psum | solution.py:90
  249.3 51.9 %all-reduce.5.cloned.1.call-done = f32[4,256,32]{1,2,0:T(8,128)} async-done(((f32[4,256,32]{1,2,0:T(8,128)}), f32[4,256,32]{1,2,0:T(8,128)}) %all-reduce.5.cloned.1.call-update) | async-done | bytes 131088 | tf_op jit(solution)/shard_map/psum | solution.py:90
  301.2 1.6 add_divide_fusion
  (44 shorter events, 9.1 us)
Async XLA Ops:
  9.4 24.8 %all-to-all-start.2 = ((f32[8,64,4]{0,2,1:T(4,128)}), f32[8,64,4]{0,2,1:T(4,128)S(1)}, u32[]{:S(2)}, u32[]{:S(2)}) async-start(f32[8,64,4]{0,2,1:T(4,128)} %broadcast_in_dim.61), calls=%async_computation.2 | async-start | bytes 262144 | tf_op jit(solution)/shard_map/all_to_all | solution.py:77
  28.1 57.1 %copy-start.2 = (bf16[128,4096]{1,0:T(8,128)(2,1)S(1)}, bf16[128,4096]{1,0:T(8,128)(2,1)}, u32[]{:S(2)}) copy-start(bf16[128,4096]{1,0:T(8,128)(2,1)} %param.7) | copy-start | bytes 3145732
  34.2 33.8 %all-to-all-start = ((f32[1024,64,4]{0,2,1:T(4,128)}), f32[1024,64,4]{0,2,1:T(4,128)S(1)}, u32[]{:S(2)}, u32[]{:S(2)}) async-start(f32[1024,64,4]{0,2,1:T(4,128)} %all_to_all.34), calls=%async_computation | async-start | bytes 2097152 | tf_op jit(solution)/shard_map/all_to_all | solution.py:76
  68.0 13.4 %all-to-all-start.3 = ((f32[8,1,256]{2,1,0:T(1,128)}), f32[8,1,256]{2,1,0:T(1,128)S(1)}, u32[]{:S(2)}, u32[]{:S(2)}) async-start(f32[8,1,256]{2,1,0:T(1,128)} %copy.26), calls=%async_computation.3 | async-start | bytes 16384 | tf_op jit(solution)/shard_map/all_to_all | solution.py:81
  74.8 11.1 %copy-start.1 = (f32[4,256,32]{1,2,0:T(8,128)S(1)}, f32[4,256,32]{1,2,0:T(8,128)}, u32[]{:S(2)}) copy-start(f32[4,256,32]{1,2,0:T(8,128)} %param.8) | copy-start | bytes 393220
  81.4 30.4 %all-to-all-start.1 = ((f32[8,128,256]{1,2,0:T(8,128)}), f32[8,128,256]{1,2,0:T(8,128)S(1)}, u32[]{:S(2)}, u32[]{:S(2)}) async-start(f32[8,128,256]{1,2,0:T(8,128)} %copy.25), calls=%async_computation.1 | async-start | bytes 2097152 | tf_op jit(solution)/shard_map/all_to_all | solution.py:80
  84.9 164.3 %all-reduce.3.cloned.1.call-start = ((), (), s32[]{:S(2)}) async-start(), calls=%async_computation.4 | async-start | bytes 262144 | tf_op jit(solution)/shard_map/psum | solution.py:90
  119.2 6.5 %copy-start = (f32[4,256,1024]{2,1,0:T(8,128)S(1)}, f32[4,256,1024]{2,1,0:T(8,128)}, u32[]{:S(2)}) copy-start(f32[4,256,1024]{2,1,0:T(8,128)} %get-tuple-element.256) | copy-start | bytes 12582916 | tf_op jit(solution)/shard_map/while
  133.0 6.5 %copy-start = (f32[4,256,1024]{2,1,0:T(8,128)S(1)}, f32[4,256,1024]{2,1,0:T(8,128)}, u32[]{:S(2)}) copy-start(f32[4,256,1024]{2,1,0:T(8,128)} %get-tuple-element.256) | copy-start | bytes 12582916 | tf_op jit(solution)/shard_map/while
  140.1 0.7 copy-start.3
  140.8 160.4 %all-reduce.5.cloned.1.call-start = ((), (), s32[]{:S(2)}) async-start(), calls=%async_computation.5 | async-start | bytes 262144 | tf_op jit(solution)/shard_map/psum | solution.py:90
Sparse Core Ops, SparseCore 0:
  140.9 108.2 all-reduce.2
  251.7 49.4 all-reduce.4
